TPU v7x, 256 devices: a whole 4x4x8 slice. The times are simulated.
256 devices in a mesh: seq: 64 (over z, x, core), head: 4 (over y).
Axes of the slice: x: 4, y: 4, z: 8, core: 2. Of those that a mesh axis runs over, the one named last changes fastest.
Arguments:
- queries: bfloat16 [4, 16384, 128], P('head', 'seq'), may hold values from -8 to 8
- keys: bfloat16 [4, 16384, 128], P('head', 'seq'), may hold values from -6 to 6
- state_b: bfloat16 [4, 16384, 128], P('head', 'seq'), may hold values from -6 to 6
- state_c: bfloat16 [4, 16384, 128], P('head', 'seq'), may hold values from -6 to 6
- decay: float32 [4, 16384], P('head', 'seq'), may hold values from -1 to 0, as said below
Outputs:
- grad_b: float32 [4, 16384, 128], P('head', 'seq')
- grad_c: float32 [4, 16384, 128], P('head', 'seq')
- grad_decay: float32 [4, 16384], P('head', 'seq')
- distance: float32 [], replicated
Inputs may be any that keep to these rules, and one draw needn't show every extreme that they name: decay is negative.
All inputs are finite; a program needn't handle non-finite values.
Results may differ from a plain program's by a relative error of at most 0.00096.
Values may be sent and summed in bfloat16 or wider, within the bound.
A program may use at most 128 MiB of HBM per device.

v0:
```python
import math
import jax
import jax.numpy as jnp
from jax import lax
from jax.sharding import PartitionSpec as P

floor_score = -1e30


def prefix(part, axis, combine, identity, reverse):
    count = lax.axis_size(axis)
    place = lax.axis_index(axis)
    ahead = count - 1 - place if reverse else place
    gathered = lax.all_gather(part, axis)
    state = jnp.zeros_like(part) + jnp.asarray(identity, part.dtype)

    def one(lap, state):
        source = count - 1 - lap if reverse else lap
        return combine(state, lax.dynamic_index_in_dim(gathered, source, 0, False))

    return lax.fori_loop(0, ahead, one, state)


def score_block(query_rows, key_rows):
    return jnp.dot(query_rows, key_rows.T, preferred_element_type=jnp.float32) / math.sqrt(
        query_rows.shape[1]
    )


def pair_block(scores, causal, log_total, cum_query, cum_key, output_rows, input_rows, weight):
    attention = jnp.where(causal, jnp.exp(scores - log_total[:, None]), 0.0)
    spread = jnp.where(
        causal, jnp.exp(jnp.minimum(cum_query[:, None] - cum_key[None, :], 0.0)), 0.0
    )
    student = (
        weight * spread * jnp.dot(output_rows, input_rows.T, preferred_element_type=jnp.float32)
    )
    misfit = student - attention
    return ((misfit * spread).astype(jnp.bfloat16), misfit)


def row_max_update(state_acc, query_rows, pos_query, key_rows, pos_key):
    running_max, denominator = state_acc
    scores = score_block(query_rows, key_rows)
    causal = pos_query[:, None] >= pos_key[None, :]
    new_max = jnp.maximum(running_max, jnp.max(jnp.where(causal, scores, floor_score), axis=1))
    fresh = jnp.sum(jnp.where(causal, jnp.exp(scores - new_max[:, None]), 0.0), axis=1)
    return (new_max, denominator * jnp.exp(running_max - new_max) + fresh)


def add_terms(earlier, later):
    return earlier + later


def local(queries, keys, state_b, state_c, decay):
    query_own = queries[0]
    input_own = state_b[0]
    output_own = state_c[0]
    shard_rows = query_own.shape[0]
    state_width = input_own.shape[1]
    devices = lax.axis_size("seq")
    total_rows = shard_rows * devices
    weight = 4.0 / total_rows
    row_first = lax.axis_index("seq") * shard_rows
    row_last = row_first + shard_rows - 1
    pos_query = row_first + jnp.arange(shard_rows, dtype=jnp.int32)
    local_cum = jnp.cumsum(decay[0])
    before = prefix(local_cum[-1:], "seq", add_terms, jnp.zeros((1,), jnp.float32), False)
    cum_own = local_cum + before[0]
    cum_all = lax.all_gather(cum_own[None], "seq", axis=1, tiled=True)
    start_max = (
        jnp.full((shard_rows,), floor_score, jnp.float32),
        jnp.zeros((shard_rows,), jnp.float32),
    )
    start_pairs = (jnp.zeros((shard_rows, state_width), jnp.float32), jnp.zeros((), jnp.float32))
    key_all, input_all = (
        lax.all_gather(keys, "seq", axis=1, tiled=True),
        lax.all_gather(state_b, "seq", axis=1, tiled=True),
    )
    block_rows = math.gcd(total_rows, 1024)
    block_count = row_last // block_rows + 1

    def scan_max(block_index, state_acc):
        begin_row = block_index * block_rows
        key_rows = lax.dynamic_slice_in_dim(key_all[0], begin_row, block_rows)
        pos_key = begin_row + jnp.arange(block_rows, dtype=jnp.int32)
        return row_max_update(state_acc, query_own, pos_query, key_rows, pos_key)

    running_max, denominator = lax.fori_loop(0, block_count, scan_max, start_max)
    log_total = running_max + jnp.log(denominator)

    def tile_at(begin_row):
        key_rows = lax.dynamic_slice_in_dim(key_all[0], begin_row, block_rows)
        input_rows = lax.dynamic_slice_in_dim(input_all[0], begin_row, block_rows)
        cum_key = lax.dynamic_slice_in_dim(cum_all[0], begin_row, block_rows)
        pos_key = begin_row + jnp.arange(block_rows, dtype=jnp.int32)
        scores = score_block(query_own, key_rows)
        causal = pos_query[:, None] >= pos_key[None, :]
        mixed_tile, misfit = pair_block(
            scores, causal, log_total, cum_own, cum_key, output_own, input_rows, weight
        )
        return (mixed_tile, misfit, input_rows)

    def scan_full(block_index, state_acc):
        begin_row = block_index * block_rows
        mixed_tile, misfit, input_rows = tile_at(begin_row)
        product = jnp.dot(mixed_tile.T, output_own, preferred_element_type=jnp.float32)
        current = lax.dynamic_slice_in_dim(state_acc[2], begin_row, block_rows)
        updated = lax.dynamic_update_slice_in_dim(state_acc[2], current + product, begin_row, 0)
        return (
            state_acc[0] + jnp.dot(mixed_tile, input_rows, preferred_element_type=jnp.float32),
            state_acc[1] + jnp.sum(misfit * misfit),
            updated,
        )

    start_full = (start_pairs[0], start_pairs[1], jnp.zeros((total_rows, state_width), jnp.float32))
    grad_out, square_sum, local_grad_full = lax.fori_loop(0, block_count, scan_full, start_full)
    log_total, grad_out, square_sum, grad_full = (log_total, grad_out, square_sum, local_grad_full)
    grad_in = lax.psum_scatter(grad_full, "seq", scatter_dimension=0, tiled=True)
    cum_gradient = jnp.sum(output_own.astype(jnp.float32) * grad_out, axis=1) - jnp.sum(
        input_own.astype(jnp.float32) * grad_in, axis=1
    )
    behind = jnp.flip(jnp.cumsum(jnp.flip(cum_gradient)))
    suffix_sum = prefix(behind[:1], "seq", add_terms, jnp.zeros((1,), jnp.float32), True)
    grad_decay = ((behind + suffix_sum[0]) / math.sqrt(total_rows))[None]
    head_count = lax.axis_size("head") * queries.shape[0]
    everything = lax.psum(square_sum, ("seq", "head"))
    distance = jnp.sqrt(everything / (head_count * total_rows))
    return (grad_in[None], grad_out[None], grad_decay, distance)


def solution(mesh):
    return jax.shard_map(
        local,
        mesh=mesh,
        in_specs=(
            P("head", "seq", None),
            P("head", "seq", None),
            P("head", "seq", None),
            P("head", "seq", None),
            P("head", "seq"),
        ),
        out_specs=(P("head", "seq", None), P("head", "seq", None), P("head", "seq"), P()),
        check_vma=False,
    )
```

profile of v0, /device:TPU:8, one launch (start us, length us, event | category | flops | bytes accessed | tf_op | source)
XLA Modules:
  0.0 772.7 jit_solution(17249205068558108466)
XLA Ops:
  7.2 0.7 all-gather.7.cloned.1.call-update
  7.9 0.7 all-gather.5.cloned.1.call-update
  8.7 1.0 reduce-window.16
  9.8 1.3 dynamic-slice.4
  11.3 0.8 slice_dynamic-update-slice_fusion.1
  12.1 131.7 %all-reduce = f32[64]{0:T(128)S(1)} all-reduce(f32[64]{0:T(128)S(1)} %slice_dynamic-update-slice_fusion.1), channel_id=2, replica_groups=mesh['seq'=64,'head'=4] {'seq'}, use_global_device_ids=true, to_apply=%add | all-reduce | flops 64 | bytes 512
  143.9 117.8 %all_gather.23 = f32[1,16384]{1,0:T(1,128)S(1)} all-gather(f32[1,256]{1,0:T(1,128)S(1)} %bitcast.90), channel_id=1, replica_groups=mesh['seq'=64,'head'=4] {'seq'}, dimensions={1}, use_global_device_ids=true | all-gather | bytes 66560 | tf_op jit(solution)/shard_map/all_gather | solution.py:70
  261.6 1.6 while.52
  261.7 1.3 fusion.46
  263.4 3.5 broadcast_in_dim.40
  266.9 7.6 while.53
  266.9 1.3 fusion.55
  268.3 2.1 multiply_reduce_fusion.3
  270.4 1.3 convolution_add_fusion.3
  272.3 2.1 fusion.56
  274.5 209.6 %psum.7 = f32[]{:T(128)} all-reduce(f32[]{:T(128)} %get-tuple-element.198), channel_id=1, replica_groups=mesh['seq'=64,'head'=4] {'seq','head'}, use_global_device_ids=true, to_apply=%region_18.19 | all-reduce | flops 1 | bytes 8 | tf_op jit(solution)/shard_map/psum | solution.py:127
  484.9 73.7 %reduce-scatter.2.cloned.1.call-done = f32[256,128]{1,0:T(8,128)} async-done(((f32[16384,128]{1,0:T(8,128)}), f32[256,128]{1,0:T(8,128)}) %reduce-scatter.2.cloned.1.call-update) | async-done | bytes 131088 | tf_op jit(solution)/shard_map/reduce_scatter | solution.py:119
  558.6 1.0 fusion.26
  560.4 0.8 slice_dynamic-update-slice_fusion
  561.2 124.0 %all-reduce.1 = f32[64]{0:T(128)S(1)} all-reduce(f32[64]{0:T(128)S(1)} %slice_dynamic-update-slice_fusion), channel_id=3, replica_groups=mesh['seq'=64,'head'=4] {'seq'}, use_global_device_ids=true, to_apply=%add.1 | all-reduce | flops 64 | bytes 512
  685.2 79.2 %while.51 = (s32[]{:T(128)}, f32[1]{0:T(128)}, s32[]{:T(128)}, f32[64,1]{0,1:T(1,128)S(1)}, s32[]{:T(128)}, /*index=5*/s32[]{:T(128)}, s32[]{:T(128)}, s32[]{:T(128)}) while((s32[]{:T(128)}, f32[1]{0:T(128)}, s32[]{:T(128)}, f32[64,1]{0,1:T(1,128)S(1)}, s32[]{:T(128)}, /*index=5*/s32[]{:T(128)}, s32[]{:T(128)}, s32[]{:T(128)}) %tuple.103), condition=%wide.region_17.18_spmd, body=%wide.region_16.17_spmd.sunk | while | flops 7 | bytes 163 | solution.py:21
  687.8 0.6 constant_dynamic-slice_fusion.7
  692.8 0.6 constant_dynamic-slice_fusion.7
  706.6 0.6 constant_dynamic-slice_fusion.7
  (106 shorter events, 37.5 us)
Async XLA Ops:
  7.2 254.5 %all-gather.7.cloned.1.call-start = ((), (), s32[]{:S(2)}) async-start(), calls=%async_computation.2 | async-start | bytes 4259840 | tf_op jit(solution)/shard_map/all_gather | solution.py:77
  7.9 255.4 %all-gather.5.cloned.1.call-start = ((), (), s32[]{:S(2)}) async-start(), calls=%async_computation.1 | async-start | bytes 4259840 | tf_op jit(solution)/shard_map/all_gather | solution.py:78
  8.7 549.9 %reduce-scatter.2.cloned.1.call-start = ((), (), s32[]{:S(2)}) async-start(), calls=%async_computation.3 | async-start | bytes 8519680 | tf_op jit(solution)/shard_map/reduce_scatter | solution.py:119
  263.4 3.5 copy-start.1
  263.4 3.5 copy-start.3
  274.5 210.3 %copy-start = (f32[256,128]{1,0:T(8,128)}, f32[256,128]{1,0:T(8,128)S(1)}, u32[]{:S(2)}) copy-start(f32[256,128]{1,0:T(8,128)S(1)} %get-tuple-element.196) | copy-start | bytes 393220
  274.5 284.1 %copy-start.2 = (bf16[1,256,128]{2,1,0:T(8,128)(2,1)S(1)}, bf16[1,256,128]{2,1,0:T(8,128)(2,1)}, u32[]{:S(2)}) copy-start(bf16[1,256,128]{2,1,0:T(8,128)(2,1)} %param.15) | copy-start | bytes 196612
Sparse Core Ops, SparseCore 0:
  10.8 81.8 all-gather.6
  95.4 76.2 all-gather.4
  274.6 283.9 reduce-scatter.1
where the time goes:
time: 776 us; the launch traced here: 773 us
  blocking collectives  583 us (75%)
  waiting for transfers between devices  75.1 us (10%)
  local copies, waits for them, and re-layouts  43.8 us (6%)
  loops' own time  43.1 us (6%)
  between operations  15.7 us (2%)
  matrix products  8.2 us (1%)
    unnamed x2, blocking collectives  256 us
    psum x1, blocking collectives, local(): everything = lax.psum(square_sum, ('seq', 'head'))  210 us
    all_gather x1, blocking collectives, local(): cum_all = lax.all_gather(cum_own[None], 'seq', axis=1, tiled=True)  118 us
    reduce_scatter x1, waiting for transfers between devices, local(): lax.psum_scatter(grad_full, 'seq', scatter_dimension=0, tiled=True)  73.7 us
    another operation x2, loops' own time, prefix(): return lax.fori_loop(0, ahead, one, state)  42.4 us
    dynamic_slice x63, local copies, waits for them, and re-layouts, one(): return combine(state, lax.dynamic_index_in_dim(gathered, source, 0, False))  36.9 us
  transfers between devices with their start and end apart: 3, of which 1 were waited for; matrix products, arithmetic and copies ran while one was open for 1% of the time, Pallas kernels for 0%

commit v1 on v0

--- a/solution.py
+++ b/solution.py
@@ -67,7 +67,11 @@
     local_cum = jnp.cumsum(decay[0])
     before = prefix(local_cum[-1:], "seq", add_terms, jnp.zeros((1,), jnp.float32), False)
     cum_own = local_cum + before[0]
-    cum_all = lax.all_gather(cum_own[None], "seq", axis=1, tiled=True)
+    own = cum_own[None]
+    devices_2 = lax.axis_size("seq")
+    blocks = jnp.stack([own for _ in range(devices_2)])
+    blocks = lax.all_to_all(blocks, "seq", split_axis=0, concat_axis=0)
+    cum_all = jnp.concatenate(blocks, axis=1)
     start_max = (
         jnp.full((shard_rows,), floor_score, jnp.float32),
         jnp.zeros((shard_rows,), jnp.float32),

time: 776 us -> 744 us (0.959)
  blocking collectives: 583 us -> 461 us
  starting transfers between devices: 0.11 us -> 81.1 us
  waiting for transfers between devices: 75.1 us -> 83.7 us
    all_gather x1 -> x0, blocking collectives: 118 us -> none  [local(): cum_all = lax.all_gather(cum_own[None], 'seq', axis=1, tiled=True)]
    all_to_all x0 -> x1, starting transfers between devices: none -> 81 us  [local(): blocks = lax.all_to_all(blocks, 'seq', split_axis=0, concat_axis=0)]
    all_to_all x0 -> x1, waiting for transfers between devices: none -> 8.25 us  [local(): blocks = lax.all_to_all(blocks, 'seq', split_axis=0, concat_axis=0)]
  transfers between devices with their start and end apart: 3 -> 4, of which waited for: 1 -> 2; matrix products, arithmetic and copies ran while one was open for 1% -> 1% of each run, Pallas kernels for 0% -> 0%
where the time goes in v1:
time: 744 us; the launch traced here: 741 us
  blocking collectives  461 us (62%)
  waiting for transfers between devices  83.7 us (11%)
  starting transfers between devices  81.1 us (11%)
  local copies, waits for them, and re-layouts  44.7 us (6%)
  loops' own time  43.1 us (6%)
  between operations  15.7 us (2%)
  matrix products  8.17 us (1%)
    unnamed x2, blocking collectives  256 us
    psum x1, blocking collectives, local(): everything = lax.psum(square_sum, ('seq', 'head'))  205 us
    all_to_all x1, starting transfers between devices, local(): blocks = lax.all_to_all(blocks, 'seq', split_axis=0, concat_axis=0)  81 us
    reduce_scatter x1, waiting for transfers between devices, local(): lax.psum_scatter(grad_full, 'seq', scatter_dimension=0, tiled=True)  74 us
    another operation x2, loops' own time, prefix(): return lax.fori_loop(0, ahead, one, state)  42.4 us
    dynamic_slice x63, local copies, waits for them, and re-layouts, one(): return combine(state, lax.dynamic_index_in_dim(gathered, source, 0, False))  36.9 us
  transfers between devices with their start and end apart: 4, of which 2 were waited for; matrix products, arithmetic and copies ran while one was open for 1% of the time, Pallas kernels for 0%

profile of v1, /device:TPU:8, one launch (start us, length us, event | category | flops | bytes accessed | tf_op | source)
XLA Modules:
  0.0 740.8 jit_solution(16685354268090047766)
XLA Ops:
  7.2 0.7 all-gather.7.cloned.1.call-update
  7.9 0.7 all-gather.5.cloned.1.call-update
  8.7 1.0 reduce-window.16
  9.8 1.3 dynamic-slice.3
  11.3 0.9 slice_dynamic-update-slice_fusion.1
  12.1 131.7 %all-reduce = f32[64]{0:T(128)S(1)} all-reduce(f32[64]{0:T(128)S(1)} %slice_dynamic-update-slice_fusion.1), channel_id=2, replica_groups=mesh['seq'=64,'head'=4] {'seq'}, use_global_device_ids=true, to_apply=%add | all-reduce | flops 64 | bytes 512
  143.8 0.7 stack.3
  144.5 81.0 %all-to-all-start = ((f32[64,1,256]{2,1,0:T(1,128)}), f32[64,1,256]{2,1,0:T(1,128)S(1)}, u32[]{:S(2)}, u32[]{:S(2)}) async-start(f32[64,1,256]{2,1,0:T(1,128)} %stack.3), calls=%async_computation | async-start | bytes 131072 | tf_op jit(solution)/shard_map/all_to_all | solution.py:73
  225.6 1.7 while.52
  225.6 1.3 fusion.46
  227.3 8.3 %all-to-all-done = f32[64,1,256]{2,1,0:T(1,128)S(1)} async-done(((f32[64,1,256]{2,1,0:T(1,128)}), f32[64,1,256]{2,1,0:T(1,128)S(1)}, u32[]{:S(2)}, u32[]{:S(2)}) %all-to-all-start) | async-done | bytes 65568 | tf_op jit(solution)/shard_map/all_to_all | solution.py:73
  235.6 3.5 broadcast_in_dim.39
  239.1 7.6 %while.53 = (s32[]{:T(128)}, f32[256,128]{1,0:T(8,128)S(1)}, f32[]{:T(128)}, f32[16384,128]{1,0:T(8,128)}, s32[]{:T(128)}, /*index=5*/f32[256]{0:T(256)S(1)}, f3...) while((s32[]{:T(128)}, f32[256,128]{1,0:T(8,128)S(1)}, ...), condition=%wide.region_10.11_spmd.clone, body=%wide.region_8.10_spmd.clone.sunk | while | flops 272532736 | bytes 5993727 | solution.py:121
  239.1 1.3 fusion.55
  240.4 2.1 multiply_reduce_fusion.3
  242.5 1.3 convolution_add_fusion.3
  244.5 2.1 fusion.56
  246.7 205.1 %psum.7 = f32[]{:T(128)} all-reduce(f32[]{:T(128)} %get-tuple-element.198), channel_id=1, replica_groups=mesh['seq'=64,'head'=4] {'seq','head'}, use_global_device_ids=true, to_apply=%region_18.19 | all-reduce | flops 1 | bytes 8 | tf_op jit(solution)/shard_map/psum | solution.py:131
  452.5 74.0 %reduce-scatter.2.cloned.1.call-done = f32[256,128]{1,0:T(8,128)} async-done(((f32[16384,128]{1,0:T(8,128)}), f32[256,128]{1,0:T(8,128)}) %reduce-scatter.2.cloned.1.call-update) | async-done | bytes 131088 | tf_op jit(solution)/shard_map/reduce_scatter | solution.py:123
  526.6 1.0 fusion.26
  528.4 0.9 slice_dynamic-update-slice_fusion
  529.3 124.0 %all-reduce.1 = f32[64]{0:T(128)S(1)} all-reduce(f32[64]{0:T(128)S(1)} %slice_dynamic-update-slice_fusion), channel_id=3, replica_groups=mesh['seq'=64,'head'=4] {'seq'}, use_global_device_ids=true, to_apply=%add.1 | all-reduce | flops 64 | bytes 512
  653.3 79.2 %while.51 = (s32[]{:T(128)}, f32[1]{0:T(128)}, s32[]{:T(128)}, f32[64,1]{0,1:T(1,128)S(1)}, s32[]{:T(128)}, /*index=5*/s32[]{:T(128)}, s32[]{:T(128)}, s32[]{:T(128)}) while((s32[]{:T(128)}, f32[1]{0:T(128)}, s32[]{:T(128)}, f32[64,1]{0,1:T(1,128)S(1)}, s32[]{:T(128)}, /*index=5*/s32[]{:T(128)}, s32[]{:T(128)}, s32[]{:T(128)}) %tuple.103), condition=%wide.region_17.18_spmd, body=%wide.region_16.17_spmd.sunk | while | flops 7 | bytes 163 | solution.py:21
  654.6 0.6 constant_dynamic-slice_fusion.5
  (107 shorter events, 38.6 us)
Async XLA Ops:
  7.2 218.4 %all-gather.7.cloned.1.call-start = ((), (), s32[]{:S(2)}) async-start(), calls=%async_computation.3 | async-start | bytes 4259840 | tf_op jit(solution)/shard_map/all_gather | solution.py:81
  7.9 227.6 %all-gather.5.cloned.1.call-start = ((), (), s32[]{:S(2)}) async-start(), calls=%async_computation.2 | async-start | bytes 4259840 | tf_op jit(solution)/shard_map/all_gather | solution.py:82
  144.5 91.0 %all-to-all-start = ((f32[64,1,256]{2,1,0:T(1,128)}), f32[64,1,256]{2,1,0:T(1,128)S(1)}, u32[]{:S(2)}, u32[]{:S(2)}) async-start(f32[64,1,256]{2,1,0:T(1,128)} %stack.3), calls=%async_computation | async-start | bytes 131072 | tf_op jit(solution)/shard_map/all_to_all | solution.py:73
  225.5 301.1 %reduce-scatter.2.cloned.1.call-start = ((), (), s32[]{:S(2)}) async-start(), calls=%async_computation.4 | async-start | bytes 8519680 | tf_op jit(solution)/shard_map/reduce_scatter | solution.py:123
  235.5 3.5 copy-start.1
  235.5 3.5 copy-start.3
  246.6 205.8 %copy-start = (f32[256,128]{1,0:T(8,128)}, f32[256,128]{1,0:T(8,128)S(1)}, u32[]{:S(2)}) copy-start(f32[256,128]{1,0:T(8,128)S(1)} %get-tuple-element.196) | copy-start | bytes 393220
  246.6 279.9 %copy-start.2 = (bf16[1,256,128]{2,1,0:T(8,128)(2,1)S(1)}, bf16[1,256,128]{2,1,0:T(8,128)(2,1)}, u32[]{:S(2)}) copy-start(bf16[1,256,128]{2,1,0:T(8,128)(2,1)} %param.15) | copy-start | bytes 196612
Sparse Core Ops, SparseCore 0:
  10.8 81.9 all-gather.6
  95.5 76.2 all-gather.4
  246.8 279.7 reduce-scatter.1
